TPU v7x, 256 devices: a whole 4x4x8 slice. The times are simulated.
256 devices in a mesh: frames: 64 (over z, y, core), heads: 4 (over x).
Axes of the slice: x: 4, y: 4, z: 8, core: 2. Of those that a mesh axis runs over, the one named last changes fastest.
Arguments:
- query_in: bfloat16 [8192, 5120], P(('frames', 'heads')), may hold values from -6 to 6
- key_in: bfloat16 [8192, 5120], P(('frames', 'heads')), may hold values from -6 to 6
- value_in: bfloat16 [8192, 5120], P(('frames', 'heads')), may hold values from -6 to 6
- query_gain: float32 [5120], replicated, may hold values from 1.2 to 8
- key_gain: float32 [5120], replicated, may hold values from 1.2 to 8
- keep_flags: int32 [64, 64], P('frames'), may hold values from 0 to 1, as said below
- pool_levels: int32 [64, 64], P('frames'), may hold values from 0 to 3, as said below
- live_counts: int32 [64], replicated, may hold values from 64 to 128, as said below
Outputs:
- attended: bfloat16 [8192, 5120], P(('frames', 'heads'))
Inputs may be any that keep to these rules, and one draw needn't show every extreme that they name: keep_flags[i, i] = 1; for j - i = +-2^k with k < 3 an entry is 0 or 1; all others are 0. For j - i = +-2^k with k < 3, pool_levels[i, j] is k or k + 1; all others are 0. `live_counts`: some frame has all of its tokens live.
All inputs are finite; a program needn't handle non-finite values.
Results may differ from a plain program's by a relative error of at most 0.01.
The roundings to bfloat16 on the way count: a program that leaves them out, or rounds other values in their place, can miss the bound.
Values may be sent and summed in bfloat16 or wider, within the bound.
No kernel may reach another device: no remote copies, remote signals or barrier semaphores. Data moves between devices by JAX's collectives and lax.ppermute only.
A program may use at most 128 MiB of HBM per device.

v0:
```python
import math

import jax
import jax.numpy as jnp
import numpy as np
from jax import lax
from jax.experimental import pallas as pl
from jax.experimental.pallas import tpu as pltpu
from jax.sharding import PartitionSpec as P

HDIM = 128
PW = 32
LEVELS = 3
EPSILON = 1e-06
FLOOR = -1e30
LOG2E = math.log2(math.e)


def frequency_rows():
    half = HDIM // 2
    third = half // 3
    lead = half - 2 * third
    rows = np.zeros((8, HDIM), np.float64)
    for lane in range(HDIM):
        i = lane // 2
        if i < lead:
            rows[0, lane] = 10000.0 ** (-i / lead)
        elif i < lead + third:
            rows[1, lane] = 10000.0 ** (-(i - lead) / third)
        else:
            rows[2, lane] = 10000.0 ** (-(i - lead - third) / third)
    return rows.astype(np.float32)


def rotary_tables(rows, freq):
    frame = lax.axis_index("frames")
    token = lax.axis_index("heads") * rows + lax.broadcasted_iota(jnp.int32, (rows, HDIM), 0)
    even = lax.broadcasted_iota(jnp.int32, (rows, HDIM), 1) % 2 == 0
    angles = (
        frame.astype(jnp.float32) * freq[0:1]
        + (token // PW).astype(jnp.float32) * freq[1:2]
        + (token % PW).astype(jnp.float32) * freq[2:3]
    )
    sine = jnp.sin(angles)
    return jnp.cos(angles), jnp.where(even, -sine, sine), even


def steps_of(count):
    return (0, *range(count - 1, 0, -1))


def block_bases(count, width):
    own_part = lax.axis_index("heads")
    return [pl.multiple_of((own_part ^ step) * width, width) for step in steps_of(count)]


def turn(x_ref, gain_ref, tables, stores, part_width):
    cosine, sine, even = tables
    floats = x_ref[...].astype(jnp.float32)
    inverse = lax.rsqrt(jnp.mean(floats * floats, axis=1, keepdims=True) + EPSILON)
    for base, store in zip(block_bases(len(stores), part_width), stores):
        for offset in range(0, part_width, HDIM):
            at = pl.ds(pl.multiple_of(base + offset, HDIM), HDIM)
            scaled = x_ref[:, at].astype(jnp.float32) * inverse * gain_ref[:, at]
            partner = jnp.where(even, pltpu.roll(scaled, HDIM - 1, 1), pltpu.roll(scaled, 1, 1))
            store(offset, (scaled * cosine + partner * sine).astype(jnp.bfloat16))


def store_in(ref):
    def store(offset, values):
        ref[:, offset : offset + HDIM] = values

    return store


def prepare_kernel(live_hbm, k_hbm, v_hbm, kg_hbm, freq_hbm, q_hbm, qg_hbm, *rest):
    (*block_refs, early_ref, qo_ref, k_ref, kg_ref, freq_ref, q_ref, qg_ref) = rest[:-3]
    live_ref, arrived, placed = rest[-3:]
    rows, width = k_ref.shape
    part_width = width // len(block_refs)
    bases = block_bases(len(block_refs), part_width)
    copies = [
        pltpu.make_async_copy(source, target, arrived.at[number])
        for number, (source, target) in enumerate(
            (
                (freq_hbm, freq_ref),
                (k_hbm, k_ref),
                (kg_hbm, kg_ref),
                (q_hbm, q_ref),
                (qg_hbm, qg_ref),
                (live_hbm, live_ref),
            )
        )
    ]
    copies += [
        pltpu.make_async_copy(
            v_hbm.at[:, pl.ds(base, part_width)],
            block_ref.at[:, part_width:],
            placed.at[step],
        )
        for step, (base, block_ref) in enumerate(zip(bases, block_refs))
    ]
    for copy in copies:
        copy.start()
    copies[0].wait()
    tables = rotary_tables(rows, freq_ref[...])
    copies[1].wait()
    copies[2].wait()
    turn(k_ref, kg_ref, tables, [store_in(ref) for ref in block_refs], part_width)
    for copy in copies[3:]:
        copy.wait()
    live = pick(live_ref, lax.axis_index("frames")) - lax.axis_index("heads") * rows
    for base, block_ref in zip(bases, block_refs):
        two = pooled_floats(pooled(block_ref[...], live, 0), live, 1)
        both = jnp.concatenate([two[:, :part_width], two[:, part_width:]], axis=0)
        early_ref[:, pl.ds(base, part_width)] = both.astype(jnp.bfloat16)
    turn(
        q_ref,
        qg_ref,
        tables,
        [store_in(qo_ref.at[step]) for step in range(len(block_refs))],
        part_width,
    )


def source_of(frame, slot):
    odd = frame % 2
    if slot == "cross":
        return ((frame + 1) ^ 1) - 1
    if slot == "chip":
        return frame ^ 1
    if slot == "ahead":
        return frame + 4 * odd - 2
    if slot == "handed":
        return frame - 4 * odd + 2
    if slot == "four":
        return frame ^ 4
    return ((frame + 4) ^ 4) - 4


def pick(row_ref, index):
    row = row_ref[...]
    lane = lax.broadcasted_iota(jnp.int32, row.shape, 1)
    chosen = jnp.where(lane == index, row, 0).astype(jnp.float32)
    return jnp.sum(chosen, axis=1, keepdims=True).astype(jnp.int32)


def weights_of(live, index, group):
    return jnp.clip(live - index * group, 0, group)


def pooled_floats(values, live, level):
    count = values.shape[0]
    half = count // 2
    group = 2**level
    out_row = lax.broadcasted_iota(jnp.int32, (half, count), 0)
    in_row = lax.broadcasted_iota(jnp.int32, (half, count), 1)
    mix = jnp.where(in_row // 2 == out_row, weights_of(live, in_row, group), 0)
    total = weights_of(live, lax.broadcasted_iota(jnp.int32, (half, 1), 0), 2 * group)
    summed = jnp.dot(
        mix.astype(jnp.float32).astype(jnp.bfloat16), values, preferred_element_type=jnp.float32
    )
    return summed * (1.0 / jnp.maximum(total, 1).astype(jnp.float32))


def pooled(values, live, level):
    return pooled_floats(values, live, level).astype(jnp.bfloat16)


def assemble_kernel(*refs):
    block_refs, own_ref = refs[:-1], refs[-1]
    rows = block_refs[0].shape[0]
    for first, block_ref in zip(block_bases(len(block_refs), rows), block_refs):
        own_ref[pl.ds(first, rows), :] = block_ref[...]


def pool_kernel(live_ref, own_ref, one_ref):
    one_ref[...] = pooled(own_ref[...], pick(live_ref, lax.axis_index("frames")), 0)


def pool_cross_kernel(live_ref, far_ref, out_ref):
    source = source_of(lax.axis_index("frames"), "cross")
    out_ref[...] = pooled(far_ref[...], pick(live_ref, source), 0)


def pack_kernel(four_ref, back_ref, q_ref, *out_refs):
    parts, rows, width = q_ref.shape
    count = four_ref.shape[0]
    for step, (base, out_ref) in enumerate(zip(block_bases(parts, width), out_refs)):
        out_ref[:rows, :] = q_ref[step]
        out_ref[rows : rows + count, :] = four_ref[:, pl.ds(base, width)]
        out_ref[rows + count :, :] = back_ref[:, pl.ds(base, width)]


def selection(in_index, valid, shape, live, level, chosen):
    out_row = lax.broadcasted_iota(jnp.int32, shape, 0)
    group = 2**level
    stay = jnp.where(chosen == level, 1, 0)
    same = jnp.where(in_index == out_row, 1, 0)
    pairs = jnp.where(in_index // 2 == out_row, weights_of(live, in_index, group), 0)
    mix = jnp.where(valid, same * stay + pairs * (1 - stay), 0)
    total = weights_of(live, lax.broadcasted_iota(jnp.int32, (shape[0], 1), 0), 2 * group)
    total = stay + jnp.maximum(total, 1) * (1 - stay)
    return mix.astype(jnp.float32).astype(jnp.bfloat16), total.astype(jnp.float32)


def mixed(mix, values, total):
    summed = jnp.dot(mix, values, preferred_element_type=jnp.float32)
    return (summed * (1.0 / total)).astype(jnp.bfloat16)


def near_kernel(
    keep_ref, level_ref, live_ref, cross_ref, chip_ref, cross_out, chip_out, keep_out, level_out
):
    frame = lax.axis_index("frames")
    keep_out[...] = keep_ref[...]
    level_out[...] = level_ref[...]
    for slot, far_ref, out_ref in (
        ("cross", cross_ref, cross_out),
        ("chip", chip_ref, chip_out),
    ):
        source = source_of(frame, slot)
        count = far_ref.shape[0]
        in_index = lax.broadcasted_iota(jnp.int32, (count, count), 1)
        mix, total = selection(
            in_index, True, (count, count), pick(live_ref, source), 0, pick(level_ref, source)
        )
        out_ref[...] = mixed(mix, far_ref[...], total)


SLOTS = ("cross", "chip", "ahead", "handed", "four", "back")


def attend_kernel(keep_ref, level_ref, live_ref, own_ref, *rest):
    (*refs, result_ref, q_ref, kv_ref, bias_ref, early_ref) = rest
    parts = (len(refs) - 4) // 2
    far_refs, packed_refs, out_refs = refs[:4], refs[4 : 4 + parts], refs[4 + parts :]
    tokens, width = q_ref.shape
    rows = tokens // parts
    early_rows = (packed_refs[0].shape[0] - rows) // 2
    groups = early_rows // 2
    frame = lax.axis_index("frames")
    own_live = pick(live_ref, frame)

    def bias_row(live, count, group, active):
        weight = weights_of(live, lax.broadcasted_iota(jnp.int32, (8, count), 1), group)
        logs = jnp.log(jnp.maximum(weight, 1).astype(jnp.float32)) * LOG2E
        return jnp.where(weight * active > 0, logs, FLOOR)

    for first, packed_ref in zip(block_bases(parts, rows), packed_refs):
        q_ref[pl.ds(first, rows), :] = packed_ref[:rows, :]
    kv_ref[0:tokens, :] = own_ref[...]
    bias_ref[:, 0:tokens] = bias_row(own_live, tokens, 1, 1)
    at = tokens
    for number, slot in enumerate(SLOTS):
        level, kind = number // 2, number % 2
        count = tokens >> level
        source = source_of(frame, slot)
        chosen = pick(level_ref, source)
        live = pick(live_ref, source)
        kept = jnp.where(pick(keep_ref, source) == 1, 1, 0)
        low, high = jnp.where(chosen == level, 1, 0), jnp.where(chosen == level + 1, 1, 0)
        active = kept * (low + high)
        group = 2 ** (level + 1) - low * 2**level
        bias_ref[:, at : at + count] = bias_row(live, count, group, active)
        if level == 0:
            kv_ref[at : at + count, :] = far_refs[number][...]
        elif number < len(far_refs):
            in_index = lax.broadcasted_iota(jnp.int32, (count, count), 1)
            mix, total = selection(in_index, True, (count, count), live, level, chosen)
            kv_ref[at : at + count, :] = mixed(mix, far_refs[number][...], total)
        else:
            skip = rows + kind * early_rows
            for step, packed_ref in enumerate(packed_refs):
                early_ref[kind, step * early_rows : (step + 1) * early_rows, :] = packed_ref[
                    skip : skip + early_rows, :
                ]
            shape = (count, parts * early_rows)
            in_row = lax.broadcasted_iota(jnp.int32, shape, 1)
            inner = in_row % early_rows
            block = in_row // early_rows
            step = jnp.where(block == 0, 0, parts - block)
            part = step ^ lax.axis_index("heads")
            in_index = part * groups + inner % groups
            for half in range(2):
                valid = inner // groups == half
                mix, total = selection(in_index, valid, shape, live, level, chosen)
                kv_ref[at : at + count, half * width : (half + 1) * width] = mixed(
                    mix, early_ref[kind], total
                )
        at += count
    bias = bias_ref[0:1, :]
    alive = lax.broadcasted_iota(jnp.int32, (tokens, 1), 0) < own_live
    heads = width // HDIM
    columns = [slice(head * HDIM, (head + 1) * HDIM) for head in range(heads)]

    def scored(head):
        scores = lax.dot_general(
            q_ref[:, columns[head]],
            kv_ref[:, columns[head]],
            (((1,), (1,)), ((), ())),
            preferred_element_type=jnp.float32,
        )
        return scores * (LOG2E / math.sqrt(HDIM)) + bias

    def summed(head, probs, inverse):
        numerator = jnp.dot(
            probs,
            kv_ref[:, width + head * HDIM : width + (head + 1) * HDIM],
            preferred_element_type=jnp.float32,
        )
        result = jnp.where(alive, numerator * inverse, 0.0)
        result_ref[:, columns[head]] = result.astype(jnp.bfloat16)

    scores, waiting = scored(0), None
    for head in range(heads):
        following = scored(head + 1) if head + 1 < heads else None
        if waiting is not None:
            summed(*waiting)
        probs = jnp.exp2(scores - jnp.max(scores, axis=1, keepdims=True))
        inverse = 1.0 / jnp.sum(probs, axis=1, keepdims=True)
        waiting = (head, probs.astype(jnp.bfloat16), inverse)
        scores = following
    summed(*waiting)
    for first, out_ref in zip(block_bases(parts, rows), out_refs):
        out_ref[...] = result_ref[pl.ds(first, rows), :]


def place_kernel(*refs):
    block_refs, (out_ref, placed) = refs[:-2], refs[-2:]
    width = block_refs[0].shape[1]
    copies = [
        pltpu.make_async_copy(block_ref, out_ref.at[:, pl.ds(base, width)], placed.at[step])
        for step, (base, block_ref) in enumerate(
            zip(block_bases(len(block_refs), width), block_refs)
        )
    ]
    for copy in copies:
        copy.start()
    for copy in copies:
        copy.wait()


def shards(query_in, key_in, value_in, query_gain, key_gain, keep_flags, pool_levels, live_counts):
    rows, features = query_in.shape
    parts = lax.axis_size("heads")
    frames = lax.axis_size("frames")
    tokens = rows * parts
    width = features // parts
    vmem = pl.BlockSpec(memory_space=pltpu.VMEM)
    live_row = live_counts.reshape(1, frames)
    params = pltpu.CompilerParams(vmem_limit_bytes=32 * 2**20)
    alone = pltpu.CompilerParams(vmem_limit_bytes=60 * 2**20)
    bf16 = jnp.bfloat16

    anywhere = pl.BlockSpec(memory_space=pl.ANY)
    early_rows = 2 * rows >> (LEVELS - 1)
    floats = jnp.float32
    freq = jnp.asarray(frequency_rows())

    def array(*shape):
        return jax.ShapeDtypeStruct(shape, bf16)

    *blocks, early, query_blocks = pl.pallas_call(
        prepare_kernel,
        out_shape=[array(rows, 2 * width)] * parts
        + [array(early_rows, features), array(parts, rows, width)],
        in_specs=[anywhere] * 7,
        out_specs=[vmem] * (parts + 2),
        scratch_shapes=[
            pltpu.VMEM((rows, features), bf16),
            pltpu.VMEM((1, features), floats),
            pltpu.VMEM((8, HDIM), floats),
            pltpu.VMEM((rows, features), bf16),
            pltpu.VMEM((1, features), floats),
            pltpu.VMEM((1, frames), jnp.int32),
            pltpu.SemaphoreType.DMA((6,)),
            pltpu.SemaphoreType.DMA((parts,)),
        ],
        compiler_params=alone,
        name="prepare",
    )(
        live_row,
        key_in,
        value_in,
        key_gain.reshape(1, features),
        freq,
        query_in,
        query_gain.reshape(1, features),
    )

    def permuted(values, slot):
        pairs = []
        for frame in range(frames):
            source = source_of(frame, slot)
            for part in range(parts):
                there = frame * parts + part
                if 0 <= source < frames:
                    pairs.append((source * parts + part, there))
                elif slot == "ahead":
                    pairs.append(((frame ^ 1) * parts + part, there))
                else:
                    pairs.append((frame * parts + (part ^ 1), there))
        return lax.ppermute(values, ("frames", "heads"), pairs)

    def over_parts(blocks):
        return [blocks[0]] + [
            lax.ppermute(block, "heads", [(i, i ^ step) for i in range(parts)])
            for step, block in zip(steps_of(parts)[1:], blocks[1:])
        ]

    blocks = over_parts(blocks)
    four, back = permuted(early, "four"), permuted(early, "back")
    own = pl.pallas_call(
        assemble_kernel,
        out_shape=array(tokens, 2 * width),
        in_specs=[vmem] * parts,
        out_specs=vmem,
        compiler_params=params,
        name="assemble",
    )(*blocks)
    own, four, back = lax.optimization_barrier((own, four, back))
    cross, chip = permuted(own, "cross"), permuted(own, "chip")
    one = pl.pallas_call(
        pool_kernel,
        out_shape=array(tokens // 2, 2 * width),
        in_specs=[vmem, vmem],
        out_specs=vmem,
        compiler_params=params,
        name="pool",
    )(live_row, own)
    ahead = permuted(one, "ahead")
    four, back, chip = lax.optimization_barrier((four, back, chip))
    packed = pl.pallas_call(
        pack_kernel,
        out_shape=[array(rows + 2 * early_rows, width)] * parts,
        in_specs=[vmem] * 3,
        out_specs=[vmem] * parts,
        compiler_params=params,
        name="pack",
    )(four, back, query_blocks)
    packed = over_parts(packed)

    cross, *packed = lax.optimization_barrier((cross, *packed))
    cross_one = pl.pallas_call(
        pool_cross_kernel,
        out_shape=jax.ShapeDtypeStruct((tokens // 2, 2 * width), bf16),
        in_specs=[vmem, vmem],
        out_specs=vmem,
        compiler_params=params,
        name="pool_cross",
    )(live_row, cross)
    handed = permuted(cross_one, "chip")
    cross, chip, keep_row, level_row = pl.pallas_call(
        near_kernel,
        out_shape=[array(tokens, 2 * width)] * 2
        + [jax.ShapeDtypeStruct((1, frames), jnp.int32)] * 2,
        in_specs=[vmem] * 5,
        out_specs=[vmem] * 4,
        compiler_params=params,
        name="near",
    )(keep_flags, pool_levels, live_row, cross, chip)
    far = (cross, chip, ahead, handed)
    count = tokens + 2 * sum(tokens >> level for level in range(LEVELS))
    attended = pl.pallas_call(
        attend_kernel,
        out_shape=[array(rows, width)] * parts,
        in_specs=[vmem] * (4 + len(far) + parts),
        out_specs=[vmem] * parts,
        scratch_shapes=[
            pltpu.VMEM((tokens, width), bf16),
            pltpu.VMEM((tokens, width), bf16),
            pltpu.VMEM((count, 2 * width), bf16),
            pltpu.VMEM((8, count), jnp.float32),
            pltpu.VMEM((2, parts * early_rows, width), bf16),
        ],
        compiler_params=params,
        name="attend",
    )(keep_row, level_row, live_row, own, *far, *packed)
    return pl.pallas_call(
        place_kernel,
        out_shape=array(rows, features),
        in_specs=[vmem] * parts,
        out_specs=anywhere,
        scratch_shapes=[pltpu.SemaphoreType.DMA((parts,))],
        compiler_params=params,
        name="place",
    )(*over_parts(attended))


def solution(mesh):
    placed = (
        P(("frames", "heads"), None),
        P(("frames", "heads"), None),
        P(("frames", "heads"), None),
        P(),
        P(),
        P("frames", None),
        P("frames", None),
        P(),
    )
    return jax.shard_map(
        shards, mesh=mesh, in_specs=placed, out_specs=P(("frames", "heads"), None), check_vma=False
    )
```

profile of v0, /device:TPU:248, one launch (start us, length us, event | category | flops | bytes accessed | tf_op | source)
XLA Modules:
  0.0 49.5 jit_solution(976548237517280895)
XLA Ops:
  0.0 3.2 %prepare.1 = (bf16[32,2560]{1,0:T(8,128)(2,1)}, bf16[32,2560]{1,0:T(8,128)(2,1)}, bf16[32,2560]{1,0:T(8,128)(2,1)}, bf16[32,2560]{1,0:T(8,128)(2,1)}, bf16[16,51...) custom-call(s32[1,64]{1,0:T(1,128)} %bitcast.3, bf16[32,5120]{1,0:T(8,128)(2,1)} %k_hbm.1, bf16[32,5120]{1,0:T(8,128)(2,1)} %v_hbm.1, ...), custom_call_target="tpu_custom_call" | custom-call | tf_op jit(solution)/shard_map/prepare/pallas_call | solution.py:364
  3.2 2.8 %collective-permute-start = (bf16[32,2560]{1,0:T(8,128)(2,1)}, bf16[32,2560]{1,0:T(8,128)(2,1)S(1)}, u32[]{:S(2)}, u32[]{:S(2)}) collective-permute-start(bf16[32,2560]{1,0:T(8,128)(2,1)} %get-tuple-element.35), channel_id=1, source_target_pairs={{0,3},{1,2},{2,1},{3,0},{4,7},{5,6},{6,5},{7,4},{8,11},{9,10},{10,... | collective-permute-start | bytes 491528 | tf_op jit(solution)/shard_map/ppermute | solution.py:408
  6.1 0.8 %collective-permute-start.1 = (bf16[32,2560]{1,0:T(8,128)(2,1)}, bf16[32,2560]{1,0:T(8,128)(2,1)S(1)}, u32[]{:S(2)}, u32[]{:S(2)}) collective-permute-start(bf16[32,2560]{1,0:T(8,128)(2,1)} %get-tuple-element.36), channel_id=1, source_target_pairs={{0,2},{1,3},{2,0},{3,1},{4,6},{5,7},{6,4},{7,5},{8,10},{9,11},{10,... | collective-permute-start | bytes 491528 | tf_op jit(solution)/shard_map/ppermute | solution.py:408
  6.9 0.5 %collective-permute-start.2 = (bf16[32,2560]{1,0:T(8,128)(2,1)}, bf16[32,2560]{1,0:T(8,128)(2,1)S(1)}, u32[]{:S(2)}, u32[]{:S(2)}) collective-permute-start(bf16[32,2560]{1,0:T(8,128)(2,1)} %get-tuple-element.37), channel_id=1, source_target_pairs={{0,1},{1,0},{2,3},{3,2},{4,5},{5,4},{6,7},{7,6},{8,9},{9,8},{10,11... | collective-permute-start | bytes 491528 | tf_op jit(solution)/shard_map/ppermute | solution.py:408
  7.4 1.2 %collective-permute-start.3 = (bf16[16,5120]{1,0:T(8,128)(2,1)}, bf16[16,5120]{1,0:T(8,128)(2,1)S(1)}, u32[]{:S(2)}, u32[]{:S(2)}) collective-permute-start(bf16[16,5120]{1,0:T(8,128)(2,1)} %get-tuple-element.38), channel_id=1, source_target_pairs={{16,0},{17,1},{18,2},{19,3},{20,4},{21,5},{22,6},{23,7},{24,8},{25... | collective-permute-start | bytes 491528 | tf_op jit(solution)/shard_map/ppermute | solution.py:404
  8.6 1.5 %collective-permute-start.4 = (bf16[16,5120]{1,0:T(8,128)(2,1)}, bf16[16,5120]{1,0:T(8,128)(2,1)S(1)}, u32[]{:S(2)}, u32[]{:S(2)}) collective-permute-start(bf16[16,5120]{1,0:T(8,128)(2,1)} %get-tuple-element.38), channel_id=1, source_target_pairs={{1,0},{0,1},{3,2},{2,3},{5,4},{4,5},{7,6},{6,7},{9,8},{8,9},{11,10... | collective-permute-start | bytes 491528 | tf_op jit(solution)/shard_map/ppermute | solution.py:404
  10.1 3.3 %collective-permute-done.refs_1_ = bf16[32,2560]{1,0:T(8,128)(2,1)S(1)} collective-permute-done((bf16[32,2560]{1,0:T(8,128)(2,1)}, bf16[32,2560]{1,0:T(8,128)(2,1)S(1)}, u32[]{:S(2)}, u32[]{:S(2)}) %collective-permute-start) | collective-permute-done | bytes 163872 | tf_op jit(solution)/shard_map/ppermute | solution.py:408
  13.4 1.5 %collective-permute-done.1.refs_2_ = bf16[32,2560]{1,0:T(8,128)(2,1)S(1)} collective-permute-done((bf16[32,2560]{1,0:T(8,128)(2,1)}, bf16[32,2560]{1,0:T(8,128)(2,1)S(1)}, u32[]{:S(2)}, u32[]{:S(2)}) %collective-permute-start.1) | collective-permute-done | bytes 163872 | tf_op jit(solution)/shard_map/ppermute | solution.py:408
  14.9 1.3 %collective-permute-done.2.refs_3_ = bf16[32,2560]{1,0:T(8,128)(2,1)S(1)} collective-permute-done((bf16[32,2560]{1,0:T(8,128)(2,1)}, bf16[32,2560]{1,0:T(8,128)(2,1)S(1)}, u32[]{:S(2)}, u32[]{:S(2)}) %collective-permute-start.2) | collective-permute-done | bytes 163872 | tf_op jit(solution)/shard_map/ppermute | solution.py:408
  16.2 0.0 copy-start.1
  16.2 0.9 %copy-done.1 = bf16[32,2560]{1,0:T(8,128)(2,1)S(1)} copy-done((bf16[32,2560]{1,0:T(8,128)(2,1)S(1)}, bf16[32,2560]{1,0:T(8,128)(2,1)}, u32[]{:S(2)}) %copy-start.1) | copy-done | bytes 163864
  17.1 0.0 copy-start
  17.1 0.1 assemble.1.own_ref
  17.2 0.0 collective-permute-done.3.four_ref
  17.2 1.1 %collective-permute-done.4.back_ref = bf16[16,5120]{1,0:T(8,128)(2,1)S(1)} collective-permute-done((bf16[16,5120]{1,0:T(8,128)(2,1)}, bf16[16,5120]{1,0:T(8,128)(2,1)S(1)}, u32[]{:S(2)}, u32[]{:S(2)}) %collective-permute-start.4) | collective-permute-done | bytes 163872 | tf_op jit(solution)/shard_map/ppermute | solution.py:404
  18.3 0.0 collective-permute-start.6
  18.3 0.9 %collective-permute-start.5 = (bf16[128,2560]{1,0:T(8,128)(2,1)S(1)}, bf16[128,2560]{1,0:T(8,128)(2,1)S(1)}, u32[]{:S(2)}, u32[]{:S(2)}) collective-permute-start(bf16[128,2560]{1,0:T(8,128)(2,1)S(1)} %assemble.1.own_ref), channel_id=1, source_target_pairs={{1,0},{0,1},{3,2},{2,3},{8,4},{9,5},{10,6},{11,7},{4,8},{5,9},{6,1... | collective-permute-start | bytes 1966088 | tf_op jit(solution)/shard_map/ppermute | solution.py:404
  19.2 1.2 %collective-permute-done.6.chip_ref = bf16[128,2560]{1,0:T(8,128)(2,1)S(1)} collective-permute-done((bf16[128,2560]{1,0:T(8,128)(2,1)S(1)}, bf16[128,2560]{1,0:T(8,128)(2,1)S(1)}, u32[]{:S(2)}, u32[]{:S(2)}) %collective-permute-start.6) | collective-permute-done | bytes 655392 | tf_op jit(solution)/shard_map/ppermute | solution.py:404
  20.4 0.0 copy-done
  20.4 2.8 %collective-permute-start.7 = (bf16[64,1280]{1,0:T(8,128)(2,1)S(1)}, bf16[64,1280]{1,0:T(8,128)(2,1)S(1)}, u32[]{:S(2)}, u32[]{:S(2)}) collective-permute-start(bf16[64,1280]{1,0:T(8,128)(2,1)S(1)} %get-tuple-element.46), channel_id=1, source_target_pairs={{0,3},{1,2},{2,1},{3,0},{4,7},{5,6},{6,5},{7,4},{8,11},{9,10},{10,... | collective-permute-start | bytes 491528 | tf_op jit(solution)/shard_map/ppermute | solution.py:408
  23.3 0.0 copy-start.2
  23.3 0.8 %collective-permute-start.8 = (bf16[64,1280]{1,0:T(8,128)(2,1)S(1)}, bf16[64,1280]{1,0:T(8,128)(2,1)S(1)}, u32[]{:S(2)}, u32[]{:S(2)}) collective-permute-start(bf16[64,1280]{1,0:T(8,128)(2,1)S(1)} %get-tuple-element.47), channel_id=1, source_target_pairs={{0,2},{1,3},{2,0},{3,1},{4,6},{5,7},{6,4},{7,5},{8,10},{9,11},{10,... | collective-permute-start | bytes 491528 | tf_op jit(solution)/shard_map/ppermute | solution.py:408
  24.1 0.5 %collective-permute-start.9 = (bf16[64,1280]{1,0:T(8,128)(2,1)S(1)}, bf16[64,1280]{1,0:T(8,128)(2,1)S(1)}, u32[]{:S(2)}, u32[]{:S(2)}) collective-permute-start(bf16[64,1280]{1,0:T(8,128)(2,1)S(1)} %get-tuple-element.48), channel_id=1, source_target_pairs={{0,1},{1,0},{2,3},{3,2},{4,5},{5,4},{6,7},{7,6},{8,9},{9,8},{10,11... | collective-permute-start | bytes 491528 | tf_op jit(solution)/shard_map/ppermute | solution.py:408
  24.6 0.0 copy-done.2
  24.6 0.3 pool.1
  25.0 0.1 collective-permute-start.10
  25.0 4.2 %collective-permute-done.5.cross_ref.far_ref = bf16[128,2560]{1,0:T(8,128)(2,1)S(1)} collective-permute-done((bf16[128,2560]{1,0:T(8,128)(2,1)S(1)}, bf16[128,2560]{1,0:T(8,128)(2,1)S(1)}, u32[]{:S(2)}, u32[]{:S(2)}) %collective-permute-start.5) | collective-permute-done | bytes 655392 | tf_op jit(solution)/shard_map/ppermute | solution.py:404
  29.3 0.0 collective-permute-done.7.rest_5_
  29.3 2.7 %collective-permute-done.8.rest_6_ = bf16[64,1280]{1,0:T(8,128)(2,1)S(1)} collective-permute-done((bf16[64,1280]{1,0:T(8,128)(2,1)S(1)}, bf16[64,1280]{1,0:T(8,128)(2,1)S(1)}, u32[]{:S(2)}, u32[]{:S(2)}) %collective-permute-start.8) | collective-permute-done | bytes 163872 | tf_op jit(solution)/shard_map/ppermute | solution.py:408
  31.9 1.3 %collective-permute-done.9.rest_7_ = bf16[64,1280]{1,0:T(8,128)(2,1)S(1)} collective-permute-done((bf16[64,1280]{1,0:T(8,128)(2,1)S(1)}, bf16[64,1280]{1,0:T(8,128)(2,1)S(1)}, u32[]{:S(2)}, u32[]{:S(2)}) %collective-permute-start.9) | collective-permute-done | bytes 163872 | tf_op jit(solution)/shard_map/ppermute | solution.py:408
  33.3 0.0 copy-start.3
  33.3 0.0 copy-start.4
  33.3 0.3 pool_cross.1
  33.6 2.5 %collective-permute-start.11 = (bf16[64,2560]{1,0:T(8,128)(2,1)S(1)}, bf16[64,2560]{1,0:T(8,128)(2,1)S(1)}, u32[]{:S(2)}, u32[]{:S(2)}) collective-permute-start(bf16[64,2560]{1,0:T(8,128)(2,1)S(1)} %pool_cross.1), channel_id=1, source_target_pairs={{4,0},{5,1},{6,2},{7,3},{0,4},{1,5},{2,6},{3,7},{12,8},{13,9},{14,... | collective-permute-start | bytes 983048 | tf_op jit(solution)/shard_map/ppermute | solution.py:404
  36.1 0.0 copy-done.3
  36.1 0.0 copy-done.4
  36.1 0.6 %near.1 = (bf16[128,2560]{1,0:T(8,128)(2,1)S(1)}, bf16[128,2560]{1,0:T(8,128)(2,1)S(1)}, s32[1,64]{1,0:T(1,128)S(1)}, s32[1,64]{1,0:T(1,128)S(1)}) custom-call(s32[1,64]{1,0:T(1,128)S(1)} %copy-done.3, s32[1,64]{1,0:T(1,128)S(1)} %copy-done.4, s32[1,64]{1,0:T(1,128)S(1)} %bitcast.6, bf16[128,2560]{1,0:T(8,128)(2,1)S(1)} %collective-permute-done.5.cross_ref.far_ref, ...), custom_call_target="tpu_custom_call" | custom-call | tf_op jit(solution)/shard_map/near/pallas_call | solution.py:454
  36.7 0.0 collective-permute-done.10.rest_2_
  36.7 0.6 %collective-permute-done.11.rest_3_ = bf16[64,2560]{1,0:T(8,128)(2,1)S(1)} collective-permute-done((bf16[64,2560]{1,0:T(8,128)(2,1)S(1)}, bf16[64,2560]{1,0:T(8,128)(2,1)S(1)}, u32[]{:S(2)}, u32[]{:S(2)}) %collective-permute-start.11) | collective-permute-done | bytes 327712 | tf_op jit(solution)/shard_map/ppermute | solution.py:404
  37.4 2.1 %attend.1 = (bf16[32,1280]{1,0:T(8,128)(2,1)S(1)}, bf16[32,1280]{1,0:T(8,128)(2,1)S(1)}, bf16[32,1280]{1,0:T(8,128)(2,1)S(1)}, bf16[32,1280]{1,0:T(8,128)(2,1)S(1)}) custom-call(s32[1,64]{1,0:T(1,128)S(1)} %get-tuple-element.51.keep_ref, s32[1,64]{1,0:T(1,128)S(1)} %get-tuple-element.52.level_ref, s32[1,64]{1,0:T(1,128)S(1)} %bitcast.7, ...), custom_call_target="tpu_custom_call" | custom-call | tf_op jit(solution)/shard_map/attend/pallas_call | solution.py:465
  39.5 2.4 %collective-permute-start.12 = (bf16[32,1280]{1,0:T(8,128)(2,1)S(1)}, bf16[32,1280]{1,0:T(8,128)(2,1)S(1)}, u32[]{:S(2)}, u32[]{:S(2)}) collective-permute-start(bf16[32,1280]{1,0:T(8,128)(2,1)S(1)} %get-tuple-element.60), channel_id=1, source_target_pairs={{0,3},{1,2},{2,1},{3,0},{4,7},{5,6},{6,5},{7,4},{8,11},{9,10},{10,... | collective-permute-start | bytes 245768 | tf_op jit(solution)/shard_map/ppermute | solution.py:408
  41.9 0.8 %collective-permute-start.13 = (bf16[32,1280]{1,0:T(8,128)(2,1)S(1)}, bf16[32,1280]{1,0:T(8,128)(2,1)S(1)}, u32[]{:S(2)}, u32[]{:S(2)}) collective-permute-start(bf16[32,1280]{1,0:T(8,128)(2,1)S(1)} %get-tuple-element.61), channel_id=1, source_target_pairs={{0,2},{1,3},{2,0},{3,1},{4,6},{5,7},{6,4},{7,5},{8,10},{9,11},{10,... | collective-permute-start | bytes 245768 | tf_op jit(solution)/shard_map/ppermute | solution.py:408
  42.7 1.0 %collective-permute-start.14 = (bf16[32,1280]{1,0:T(8,128)(2,1)S(1)}, bf16[32,1280]{1,0:T(8,128)(2,1)S(1)}, u32[]{:S(2)}, u32[]{:S(2)}) collective-permute-start(bf16[32,1280]{1,0:T(8,128)(2,1)S(1)} %get-tuple-element.62), channel_id=1, source_target_pairs={{0,1},{1,0},{2,3},{3,2},{4,5},{5,4},{6,7},{7,6},{8,9},{9,8},{10,11... | collective-permute-start | bytes 245768 | tf_op jit(solution)/shard_map/ppermute | solution.py:408
  43.7 2.0 %collective-permute-done.12.refs_1_ = bf16[32,1280]{1,0:T(8,128)(2,1)S(1)} collective-permute-done((bf16[32,1280]{1,0:T(8,128)(2,1)S(1)}, bf16[32,1280]{1,0:T(8,128)(2,1)S(1)}, u32[]{:S(2)}, u32[]{:S(2)}) %collective-permute-start.12) | collective-permute-done | bytes 81952 | tf_op jit(solution)/shard_map/ppermute | solution.py:408
  45.7 3.0 %collective-permute-done.13.refs_2_ = bf16[32,1280]{1,0:T(8,128)(2,1)S(1)} collective-permute-done((bf16[32,1280]{1,0:T(8,128)(2,1)S(1)}, bf16[32,1280]{1,0:T(8,128)(2,1)S(1)}, u32[]{:S(2)}, u32[]{:S(2)}) %collective-permute-start.13) | collective-permute-done | bytes 81952 | tf_op jit(solution)/shard_map/ppermute | solution.py:408
  48.7 0.0 collective-permute-done.14.refs_3_
  48.7 0.8 %place.1 = bf16[32,5120]{1,0:T(8,128)(2,1)} custom-call(bf16[32,1280]{1,0:T(8,128)(2,1)S(1)} %get-tuple-element.59.refs_0_, bf16[32,1280]{1,0:T(8,128)(2,1)S(1)} %collective-permute-done.12.refs_1_, bf16[32,1280]{1,0:T(8,128)(2,1)S(1)} %collective-permute-done.13.refs_2_, bf16[32,1280]{1,0:T(8,128)(2,1)S(1)} %collective-permute-done.14.refs_3_), custom_call_target="tpu_custom_call" | custom-call | tf_op jit(solution)/shard_map/place/pallas_call | solution.py:480
  (1 shorter events, 0.0 us)
Async XLA Ops:
  3.2 10.2 %collective-permute-start = (bf16[32,2560]{1,0:T(8,128)(2,1)}, bf16[32,2560]{1,0:T(8,128)(2,1)S(1)}, u32[]{:S(2)}, u32[]{:S(2)}) collective-permute-start(bf16[32,2560]{1,0:T(8,128)(2,1)} %get-tuple-element.35), channel_id=1, source_target_pairs={{0,3},{1,2},{2,1},{3,0},{4,7},{5,6},{6,5},{7,4},{8,11},{9,10},{10,... | collective-permute-start | bytes 491528 | tf_op jit(solution)/shard_map/ppermute | solution.py:408
  6.1 8.8 %collective-permute-start.1 = (bf16[32,2560]{1,0:T(8,128)(2,1)}, bf16[32,2560]{1,0:T(8,128)(2,1)S(1)}, u32[]{:S(2)}, u32[]{:S(2)}) collective-permute-start(bf16[32,2560]{1,0:T(8,128)(2,1)} %get-tuple-element.36), channel_id=1, source_target_pairs={{0,2},{1,3},{2,0},{3,1},{4,6},{5,7},{6,4},{7,5},{8,10},{9,11},{10,... | collective-permute-start | bytes 491528 | tf_op jit(solution)/shard_map/ppermute | solution.py:408
  6.9 9.4 %collective-permute-start.2 = (bf16[32,2560]{1,0:T(8,128)(2,1)}, bf16[32,2560]{1,0:T(8,128)(2,1)S(1)}, u32[]{:S(2)}, u32[]{:S(2)}) collective-permute-start(bf16[32,2560]{1,0:T(8,128)(2,1)} %get-tuple-element.37), channel_id=1, source_target_pairs={{0,1},{1,0},{2,3},{3,2},{4,5},{5,4},{6,7},{7,6},{8,9},{9,8},{10,11... | collective-permute-start | bytes 491528 | tf_op jit(solution)/shard_map/ppermute | solution.py:408
  7.4 9.8 %collective-permute-start.3 = (bf16[16,5120]{1,0:T(8,128)(2,1)}, bf16[16,5120]{1,0:T(8,128)(2,1)S(1)}, u32[]{:S(2)}, u32[]{:S(2)}) collective-permute-start(bf16[16,5120]{1,0:T(8,128)(2,1)} %get-tuple-element.38), channel_id=1, source_target_pairs={{16,0},{17,1},{18,2},{19,3},{20,4},{21,5},{22,6},{23,7},{24,8},{25... | collective-permute-start | bytes 491528 | tf_op jit(solution)/shard_map/ppermute | solution.py:404
  8.6 9.7 %collective-permute-start.4 = (bf16[16,5120]{1,0:T(8,128)(2,1)}, bf16[16,5120]{1,0:T(8,128)(2,1)S(1)}, u32[]{:S(2)}, u32[]{:S(2)}) collective-permute-start(bf16[16,5120]{1,0:T(8,128)(2,1)} %get-tuple-element.38), channel_id=1, source_target_pairs={{1,0},{0,1},{3,2},{2,3},{5,4},{4,5},{7,6},{6,7},{9,8},{8,9},{11,10... | collective-permute-start | bytes 491528 | tf_op jit(solution)/shard_map/ppermute | solution.py:404
  16.2 0.9 %copy-start.1 = (bf16[32,2560]{1,0:T(8,128)(2,1)S(1)}, bf16[32,2560]{1,0:T(8,128)(2,1)}, u32[]{:S(2)}) copy-start(bf16[32,2560]{1,0:T(8,128)(2,1)} %get-tuple-element.34.refs_0_) | copy-start | bytes 491524
  17.1 3.3 %copy-start = (bf16[4,32,1280]{2,1,0:T(8,128)(2,1)S(1)}, bf16[4,32,1280]{2,1,0:T(8,128)(2,1)}, u32[]{:S(2)}) copy-start(bf16[4,32,1280]{2,1,0:T(8,128)(2,1)} %get-tuple-element.44.q_ref) | copy-start | bytes 983044
  18.3 2.1 %collective-permute-start.6 = (bf16[128,2560]{1,0:T(8,128)(2,1)S(1)}, bf16[128,2560]{1,0:T(8,128)(2,1)S(1)}, u32[]{:S(2)}, u32[]{:S(2)}) collective-permute-start(bf16[128,2560]{1,0:T(8,128)(2,1)S(1)} %assemble.1.own_ref), channel_id=1, source_target_pairs={{4,0},{5,1},{6,2},{7,3},{0,4},{1,5},{2,6},{3,7},{12,8},{13,9},{14,... | collective-permute-start | bytes 1966088 | tf_op jit(solution)/shard_map/ppermute | solution.py:404
  18.3 11.0 %collective-permute-start.5 = (bf16[128,2560]{1,0:T(8,128)(2,1)S(1)}, bf16[128,2560]{1,0:T(8,128)(2,1)S(1)}, u32[]{:S(2)}, u32[]{:S(2)}) collective-permute-start(bf16[128,2560]{1,0:T(8,128)(2,1)S(1)} %assemble.1.own_ref), channel_id=1, source_target_pairs={{1,0},{0,1},{3,2},{2,3},{8,4},{9,5},{10,6},{11,7},{4,8},{5,9},{6,1... | collective-permute-start | bytes 1966088 | tf_op jit(solution)/shard_map/ppermute | solution.py:404
  20.4 8.8 %collective-permute-start.7 = (bf16[64,1280]{1,0:T(8,128)(2,1)S(1)}, bf16[64,1280]{1,0:T(8,128)(2,1)S(1)}, u32[]{:S(2)}, u32[]{:S(2)}) collective-permute-start(bf16[64,1280]{1,0:T(8,128)(2,1)S(1)} %get-tuple-element.46), channel_id=1, source_target_pairs={{0,3},{1,2},{2,1},{3,0},{4,7},{5,6},{6,5},{7,4},{8,11},{9,10},{10,... | collective-permute-start | bytes 491528 | tf_op jit(solution)/shard_map/ppermute | solution.py:408
  23.3 1.3 %copy-start.2 = (s32[64]{0:T(128)S(1)}, s32[64]{0:T(128)}, u32[]{:S(2)}) copy-start(s32[64]{0:T(128)} %param.16) | copy-start | bytes 772
  23.3 8.6 %collective-permute-start.8 = (bf16[64,1280]{1,0:T(8,128)(2,1)S(1)}, bf16[64,1280]{1,0:T(8,128)(2,1)S(1)}, u32[]{:S(2)}, u32[]{:S(2)}) collective-permute-start(bf16[64,1280]{1,0:T(8,128)(2,1)S(1)} %get-tuple-element.47), channel_id=1, source_target_pairs={{0,2},{1,3},{2,0},{3,1},{4,6},{5,7},{6,4},{7,5},{8,10},{9,11},{10,... | collective-permute-start | bytes 491528 | tf_op jit(solution)/shard_map/ppermute | solution.py:408
  24.1 9.2 %collective-permute-start.9 = (bf16[64,1280]{1,0:T(8,128)(2,1)S(1)}, bf16[64,1280]{1,0:T(8,128)(2,1)S(1)}, u32[]{:S(2)}, u32[]{:S(2)}) collective-permute-start(bf16[64,1280]{1,0:T(8,128)(2,1)S(1)} %get-tuple-element.48), channel_id=1, source_target_pairs={{0,1},{1,0},{2,3},{3,2},{4,5},{5,4},{6,7},{7,6},{8,9},{9,8},{10,11... | collective-permute-start | bytes 491528 | tf_op jit(solution)/shard_map/ppermute | solution.py:408
  25.0 11.8 %collective-permute-start.10 = (bf16[64,2560]{1,0:T(8,128)(2,1)S(1)}, bf16[64,2560]{1,0:T(8,128)(2,1)S(1)}, u32[]{:S(2)}, u32[]{:S(2)}) collective-permute-start(bf16[64,2560]{1,0:T(8,128)(2,1)S(1)} %pool.1), channel_id=1, source_target_pairs={{4,0},{5,1},{6,2},{7,3},{12,4},{13,5},{14,6},{15,7},{0,8},{1,9},{2... | collective-permute-start | bytes 983048 | tf_op jit(solution)/shard_map/ppermute | solution.py:404
  33.3 2.9 %copy-start.3 = (s32[1,64]{1,0:T(1,128)S(1)}, s32[1,64]{1,0:T(1,128)}, u32[]{:S(2)}) copy-start(s32[1,64]{1,0:T(1,128)} %keep_ref.1) | copy-start | bytes 772
  33.3 2.9 %copy-start.4 = (s32[1,64]{1,0:T(1,128)S(1)}, s32[1,64]{1,0:T(1,128)}, u32[]{:S(2)}) copy-start(s32[1,64]{1,0:T(1,128)} %level_ref.1) | copy-start | bytes 772
  33.6 3.8 %collective-permute-start.11 = (bf16[64,2560]{1,0:T(8,128)(2,1)S(1)}, bf16[64,2560]{1,0:T(8,128)(2,1)S(1)}, u32[]{:S(2)}, u32[]{:S(2)}) collective-permute-start(bf16[64,2560]{1,0:T(8,128)(2,1)S(1)} %pool_cross.1), channel_id=1, source_target_pairs={{4,0},{5,1},{6,2},{7,3},{0,4},{1,5},{2,6},{3,7},{12,8},{13,9},{14,... | collective-permute-start | bytes 983048 | tf_op jit(solution)/shard_map/ppermute | solution.py:404
  39.5 6.2 %collective-permute-start.12 = (bf16[32,1280]{1,0:T(8,128)(2,1)S(1)}, bf16[32,1280]{1,0:T(8,128)(2,1)S(1)}, u32[]{:S(2)}, u32[]{:S(2)}) collective-permute-start(bf16[32,1280]{1,0:T(8,128)(2,1)S(1)} %get-tuple-element.60), channel_id=1, source_target_pairs={{0,3},{1,2},{2,1},{3,0},{4,7},{5,6},{6,5},{7,4},{8,11},{9,10},{10,... | collective-permute-start | bytes 245768 | tf_op jit(solution)/shard_map/ppermute | solution.py:408
  41.9 6.8 %collective-permute-start.13 = (bf16[32,1280]{1,0:T(8,128)(2,1)S(1)}, bf16[32,1280]{1,0:T(8,128)(2,1)S(1)}, u32[]{:S(2)}, u32[]{:S(2)}) collective-permute-start(bf16[32,1280]{1,0:T(8,128)(2,1)S(1)} %get-tuple-element.61), channel_id=1, source_target_pairs={{0,2},{1,3},{2,0},{3,1},{4,6},{5,7},{6,4},{7,5},{8,10},{9,11},{10,... | collective-permute-start | bytes 245768 | tf_op jit(solution)/shard_map/ppermute | solution.py:408
  42.7 6.0 %collective-permute-start.14 = (bf16[32,1280]{1,0:T(8,128)(2,1)S(1)}, bf16[32,1280]{1,0:T(8,128)(2,1)S(1)}, u32[]{:S(2)}, u32[]{:S(2)}) collective-permute-start(bf16[32,1280]{1,0:T(8,128)(2,1)S(1)} %get-tuple-element.62), channel_id=1, source_target_pairs={{0,1},{1,0},{2,3},{3,2},{4,5},{5,4},{6,7},{7,6},{8,9},{9,8},{10,11... | collective-permute-start | bytes 245768 | tf_op jit(solution)/shard_map/ppermute | solution.py:408
where the time goes:
time: 49.6 us; the launch traced here: 49.5 us
  waiting for transfers between devices  22.3 us (45%)
  starting transfers between devices  18.8 us (38%)
  Pallas kernels  7.38 us (15%)
  local copies, waits for them, and re-layouts  0.93 us (2%)
    ppermute x9, waiting for transfers between devices, over_parts(): lax.ppermute(block, 'heads', [(i, i ^ step) for i in range(parts)])  15.1 us
    ppermute x9, starting transfers between devices, over_parts(): lax.ppermute(block, 'heads', [(i, i ^ step) for i in range(parts)])  12.6 us
    ppermute x6, waiting for transfers between devices, permuted(): return lax.ppermute(values, ('frames', 'heads'), pairs)  7.21 us
    ppermute x6, starting transfers between devices, permuted(): return lax.ppermute(values, ('frames', 'heads'), pairs)  6.22 us
    pallas_call x1, Pallas kernels, shards(): pl.pallas_call(prepare_kernel, out_shape=[array(rows, 2 * width)] * parts...  3.2 us
    pallas_call x1, Pallas kernels, shards(): pl.pallas_call(attend_kernel, out_shape=[array(rows, width)] * parts, in_...  2.12 us
  transfers between devices with their start and end apart: 15, of which 11 were waited for; matrix products, arithmetic and copies ran while one was open for 0% of the time, Pallas kernels for 3%

commit v1 on v0

--- a/solution.py
+++ b/solution.py
@@ -430,7 +430,7 @@
         name="pool",
     )(live_row, own)
     ahead = permuted(one, "ahead")
-    four, back, chip = lax.optimization_barrier((four, back, chip))
+    chip, back, four = lax.optimization_barrier((chip, back, four))
     packed = pl.pallas_call(
         pack_kernel,
         out_shape=[array(rows + 2 * early_rows, width)] * parts,

time: 49.6 us -> 49.6 us (level)
  no operation moved by 1% of the time
where the time goes in v1:
time: 49.6 us; the launch traced here: 49.5 us
  waiting for transfers between devices  22.3 us (45%)
  starting transfers between devices  18.8 us (38%)
  Pallas kernels  7.38 us (15%)
  local copies, waits for them, and re-layouts  0.93 us (2%)
    ppermute x9, waiting for transfers between devices, over_parts(): lax.ppermute(block, 'heads', [(i, i ^ step) for i in range(parts)])  15.1 us
    ppermute x9, starting transfers between devices, over_parts(): lax.ppermute(block, 'heads', [(i, i ^ step) for i in range(parts)])  12.6 us
    ppermute x6, waiting for transfers between devices, permuted(): return lax.ppermute(values, ('frames', 'heads'), pairs)  7.21 us
    ppermute x6, starting transfers between devices, permuted(): return lax.ppermute(values, ('frames', 'heads'), pairs)  6.22 us
    pallas_call x1, Pallas kernels, shards(): pl.pallas_call(prepare_kernel, out_shape=[array(rows, 2 * width)] * parts...  3.2 us
    pallas_call x1, Pallas kernels, shards(): pl.pallas_call(attend_kernel, out_shape=[array(rows, width)] * parts, in_...  2.12 us
  transfers between devices with their start and end apart: 15, of which 11 were waited for; matrix products, arithmetic and copies ran while one was open for 0% of the time, Pallas kernels for 3%

profile of v1, /device:TPU:248, one launch (start us, length us, event | category | flops | bytes accessed | tf_op | source)
XLA Modules:
  0.0 49.5 jit_solution(976548237517280895)
XLA Ops:
  0.0 3.2 %prepare.1 = (bf16[32,2560]{1,0:T(8,128)(2,1)}, bf16[32,2560]{1,0:T(8,128)(2,1)}, bf16[32,2560]{1,0:T(8,128)(2,1)}, bf16[32,2560]{1,0:T(8,128)(2,1)}, bf16[16,51...) custom-call(s32[1,64]{1,0:T(1,128)} %bitcast.3, bf16[32,5120]{1,0:T(8,128)(2,1)} %k_hbm.1, bf16[32,5120]{1,0:T(8,128)(2,1)} %v_hbm.1, ...), custom_call_target="tpu_custom_call" | custom-call | tf_op jit(solution)/shard_map/prepare/pallas_call | solution.py:364
  3.2 2.8 %collective-permute-start = (bf16[32,2560]{1,0:T(8,128)(2,1)}, bf16[32,2560]{1,0:T(8,128)(2,1)S(1)}, u32[]{:S(2)}, u32[]{:S(2)}) collective-permute-start(bf16[32,2560]{1,0:T(8,128)(2,1)} %get-tuple-element.35), channel_id=1, source_target_pairs={{0,3},{1,2},{2,1},{3,0},{4,7},{5,6},{6,5},{7,4},{8,11},{9,10},{10,... | collective-permute-start | bytes 491528 | tf_op jit(solution)/shard_map/ppermute | solution.py:408
  6.1 0.8 %collective-permute-start.1 = (bf16[32,2560]{1,0:T(8,128)(2,1)}, bf16[32,2560]{1,0:T(8,128)(2,1)S(1)}, u32[]{:S(2)}, u32[]{:S(2)}) collective-permute-start(bf16[32,2560]{1,0:T(8,128)(2,1)} %get-tuple-element.36), channel_id=1, source_target_pairs={{0,2},{1,3},{2,0},{3,1},{4,6},{5,7},{6,4},{7,5},{8,10},{9,11},{10,... | collective-permute-start | bytes 491528 | tf_op jit(solution)/shard_map/ppermute | solution.py:408
  6.9 0.5 %collective-permute-start.2 = (bf16[32,2560]{1,0:T(8,128)(2,1)}, bf16[32,2560]{1,0:T(8,128)(2,1)S(1)}, u32[]{:S(2)}, u32[]{:S(2)}) collective-permute-start(bf16[32,2560]{1,0:T(8,128)(2,1)} %get-tuple-element.37), channel_id=1, source_target_pairs={{0,1},{1,0},{2,3},{3,2},{4,5},{5,4},{6,7},{7,6},{8,9},{9,8},{10,11... | collective-permute-start | bytes 491528 | tf_op jit(solution)/shard_map/ppermute | solution.py:408
  7.4 1.2 %collective-permute-start.3 = (bf16[16,5120]{1,0:T(8,128)(2,1)}, bf16[16,5120]{1,0:T(8,128)(2,1)S(1)}, u32[]{:S(2)}, u32[]{:S(2)}) collective-permute-start(bf16[16,5120]{1,0:T(8,128)(2,1)} %get-tuple-element.38), channel_id=1, source_target_pairs={{16,0},{17,1},{18,2},{19,3},{20,4},{21,5},{22,6},{23,7},{24,8},{25... | collective-permute-start | bytes 491528 | tf_op jit(solution)/shard_map/ppermute | solution.py:404
  8.6 1.5 %collective-permute-start.4 = (bf16[16,5120]{1,0:T(8,128)(2,1)}, bf16[16,5120]{1,0:T(8,128)(2,1)S(1)}, u32[]{:S(2)}, u32[]{:S(2)}) collective-permute-start(bf16[16,5120]{1,0:T(8,128)(2,1)} %get-tuple-element.38), channel_id=1, source_target_pairs={{1,0},{0,1},{3,2},{2,3},{5,4},{4,5},{7,6},{6,7},{9,8},{8,9},{11,10... | collective-permute-start | bytes 491528 | tf_op jit(solution)/shard_map/ppermute | solution.py:404
  10.1 3.3 %collective-permute-done.refs_1_ = bf16[32,2560]{1,0:T(8,128)(2,1)S(1)} collective-permute-done((bf16[32,2560]{1,0:T(8,128)(2,1)}, bf16[32,2560]{1,0:T(8,128)(2,1)S(1)}, u32[]{:S(2)}, u32[]{:S(2)}) %collective-permute-start) | collective-permute-done | bytes 163872 | tf_op jit(solution)/shard_map/ppermute | solution.py:408
  13.4 1.5 %collective-permute-done.1.refs_2_ = bf16[32,2560]{1,0:T(8,128)(2,1)S(1)} collective-permute-done((bf16[32,2560]{1,0:T(8,128)(2,1)}, bf16[32,2560]{1,0:T(8,128)(2,1)S(1)}, u32[]{:S(2)}, u32[]{:S(2)}) %collective-permute-start.1) | collective-permute-done | bytes 163872 | tf_op jit(solution)/shard_map/ppermute | solution.py:408
  14.9 1.3 %collective-permute-done.2.refs_3_ = bf16[32,2560]{1,0:T(8,128)(2,1)S(1)} collective-permute-done((bf16[32,2560]{1,0:T(8,128)(2,1)}, bf16[32,2560]{1,0:T(8,128)(2,1)S(1)}, u32[]{:S(2)}, u32[]{:S(2)}) %collective-permute-start.2) | collective-permute-done | bytes 163872 | tf_op jit(solution)/shard_map/ppermute | solution.py:408
  16.2 0.0 copy-start.1
  16.2 0.9 %copy-done.1 = bf16[32,2560]{1,0:T(8,128)(2,1)S(1)} copy-done((bf16[32,2560]{1,0:T(8,128)(2,1)S(1)}, bf16[32,2560]{1,0:T(8,128)(2,1)}, u32[]{:S(2)}) %copy-start.1) | copy-done | bytes 163864
  17.1 0.0 copy-start
  17.1 0.1 assemble.1.own_ref
  17.2 0.0 collective-permute-done.3.four_ref
  17.2 1.1 %collective-permute-done.4.back_ref = bf16[16,5120]{1,0:T(8,128)(2,1)S(1)} collective-permute-done((bf16[16,5120]{1,0:T(8,128)(2,1)}, bf16[16,5120]{1,0:T(8,128)(2,1)S(1)}, u32[]{:S(2)}, u32[]{:S(2)}) %collective-permute-start.4) | collective-permute-done | bytes 163872 | tf_op jit(solution)/shard_map/ppermute | solution.py:404
  18.3 0.0 collective-permute-start.6
  18.3 0.9 %collective-permute-start.5 = (bf16[128,2560]{1,0:T(8,128)(2,1)S(1)}, bf16[128,2560]{1,0:T(8,128)(2,1)S(1)}, u32[]{:S(2)}, u32[]{:S(2)}) collective-permute-start(bf16[128,2560]{1,0:T(8,128)(2,1)S(1)} %assemble.1.own_ref), channel_id=1, source_target_pairs={{1,0},{0,1},{3,2},{2,3},{8,4},{9,5},{10,6},{11,7},{4,8},{5,9},{6,1... | collective-permute-start | bytes 1966088 | tf_op jit(solution)/shard_map/ppermute | solution.py:404
  19.2 1.2 %collective-permute-done.6.chip_ref = bf16[128,2560]{1,0:T(8,128)(2,1)S(1)} collective-permute-done((bf16[128,2560]{1,0:T(8,128)(2,1)S(1)}, bf16[128,2560]{1,0:T(8,128)(2,1)S(1)}, u32[]{:S(2)}, u32[]{:S(2)}) %collective-permute-start.6) | collective-permute-done | bytes 655392 | tf_op jit(solution)/shard_map/ppermute | solution.py:404
  20.4 0.0 copy-done
  20.4 2.8 %collective-permute-start.7 = (bf16[64,1280]{1,0:T(8,128)(2,1)S(1)}, bf16[64,1280]{1,0:T(8,128)(2,1)S(1)}, u32[]{:S(2)}, u32[]{:S(2)}) collective-permute-start(bf16[64,1280]{1,0:T(8,128)(2,1)S(1)} %get-tuple-element.46), channel_id=1, source_target_pairs={{0,3},{1,2},{2,1},{3,0},{4,7},{5,6},{6,5},{7,4},{8,11},{9,10},{10,... | collective-permute-start | bytes 491528 | tf_op jit(solution)/shard_map/ppermute | solution.py:408
  23.3 0.0 copy-start.2
  23.3 0.8 %collective-permute-start.8 = (bf16[64,1280]{1,0:T(8,128)(2,1)S(1)}, bf16[64,1280]{1,0:T(8,128)(2,1)S(1)}, u32[]{:S(2)}, u32[]{:S(2)}) collective-permute-start(bf16[64,1280]{1,0:T(8,128)(2,1)S(1)} %get-tuple-element.47), channel_id=1, source_target_pairs={{0,2},{1,3},{2,0},{3,1},{4,6},{5,7},{6,4},{7,5},{8,10},{9,11},{10,... | collective-permute-start | bytes 491528 | tf_op jit(solution)/shard_map/ppermute | solution.py:408
  24.1 0.5 %collective-permute-start.9 = (bf16[64,1280]{1,0:T(8,128)(2,1)S(1)}, bf16[64,1280]{1,0:T(8,128)(2,1)S(1)}, u32[]{:S(2)}, u32[]{:S(2)}) collective-permute-start(bf16[64,1280]{1,0:T(8,128)(2,1)S(1)} %get-tuple-element.48), channel_id=1, source_target_pairs={{0,1},{1,0},{2,3},{3,2},{4,5},{5,4},{6,7},{7,6},{8,9},{9,8},{10,11... | collective-permute-start | bytes 491528 | tf_op jit(solution)/shard_map/ppermute | solution.py:408
  24.6 0.0 copy-done.2
  24.6 0.3 pool.1
  25.0 0.1 collective-permute-start.10
  25.0 4.2 %collective-permute-done.5.cross_ref.far_ref = bf16[128,2560]{1,0:T(8,128)(2,1)S(1)} collective-permute-done((bf16[128,2560]{1,0:T(8,128)(2,1)S(1)}, bf16[128,2560]{1,0:T(8,128)(2,1)S(1)}, u32[]{:S(2)}, u32[]{:S(2)}) %collective-permute-start.5) | collective-permute-done | bytes 655392 | tf_op jit(solution)/shard_map/ppermute | solution.py:404
  29.3 0.0 collective-permute-done.7.rest_5_
  29.3 2.7 %collective-permute-done.8.rest_6_ = bf16[64,1280]{1,0:T(8,128)(2,1)S(1)} collective-permute-done((bf16[64,1280]{1,0:T(8,128)(2,1)S(1)}, bf16[64,1280]{1,0:T(8,128)(2,1)S(1)}, u32[]{:S(2)}, u32[]{:S(2)}) %collective-permute-start.8) | collective-permute-done | bytes 163872 | tf_op jit(solution)/shard_map/ppermute | solution.py:408
  31.9 1.3 %collective-permute-done.9.rest_7_ = bf16[64,1280]{1,0:T(8,128)(2,1)S(1)} collective-permute-done((bf16[64,1280]{1,0:T(8,128)(2,1)S(1)}, bf16[64,1280]{1,0:T(8,128)(2,1)S(1)}, u32[]{:S(2)}, u32[]{:S(2)}) %collective-permute-start.9) | collective-permute-done | bytes 163872 | tf_op jit(solution)/shard_map/ppermute | solution.py:408
  33.3 0.0 copy-start.3
  33.3 0.0 copy-start.4
  33.3 0.3 pool_cross.1
  33.6 2.5 %collective-permute-start.11 = (bf16[64,2560]{1,0:T(8,128)(2,1)S(1)}, bf16[64,2560]{1,0:T(8,128)(2,1)S(1)}, u32[]{:S(2)}, u32[]{:S(2)}) collective-permute-start(bf16[64,2560]{1,0:T(8,128)(2,1)S(1)} %pool_cross.1), channel_id=1, source_target_pairs={{4,0},{5,1},{6,2},{7,3},{0,4},{1,5},{2,6},{3,7},{12,8},{13,9},{14,... | collective-permute-start | bytes 983048 | tf_op jit(solution)/shard_map/ppermute | solution.py:404
  36.1 0.0 copy-done.3
  36.1 0.0 copy-done.4
  36.1 0.6 %near.1 = (bf16[128,2560]{1,0:T(8,128)(2,1)S(1)}, bf16[128,2560]{1,0:T(8,128)(2,1)S(1)}, s32[1,64]{1,0:T(1,128)S(1)}, s32[1,64]{1,0:T(1,128)S(1)}) custom-call(s32[1,64]{1,0:T(1,128)S(1)} %copy-done.3, s32[1,64]{1,0:T(1,128)S(1)} %copy-done.4, s32[1,64]{1,0:T(1,128)S(1)} %bitcast.6, bf16[128,2560]{1,0:T(8,128)(2,1)S(1)} %collective-permute-done.5.cross_ref.far_ref, ...), custom_call_target="tpu_custom_call" | custom-call | tf_op jit(solution)/shard_map/near/pallas_call | solution.py:454
  36.7 0.0 collective-permute-done.10.rest_2_
  36.7 0.6 %collective-permute-done.11.rest_3_ = bf16[64,2560]{1,0:T(8,128)(2,1)S(1)} collective-permute-done((bf16[64,2560]{1,0:T(8,128)(2,1)S(1)}, bf16[64,2560]{1,0:T(8,128)(2,1)S(1)}, u32[]{:S(2)}, u32[]{:S(2)}) %collective-permute-start.11) | collective-permute-done | bytes 327712 | tf_op jit(solution)/shard_map/ppermute | solution.py:404
  37.4 2.1 %attend.1 = (bf16[32,1280]{1,0:T(8,128)(2,1)S(1)}, bf16[32,1280]{1,0:T(8,128)(2,1)S(1)}, bf16[32,1280]{1,0:T(8,128)(2,1)S(1)}, bf16[32,1280]{1,0:T(8,128)(2,1)S(1)}) custom-call(s32[1,64]{1,0:T(1,128)S(1)} %get-tuple-element.51.keep_ref, s32[1,64]{1,0:T(1,128)S(1)} %get-tuple-element.52.level_ref, s32[1,64]{1,0:T(1,128)S(1)} %bitcast.7, ...), custom_call_target="tpu_custom_call" | custom-call | tf_op jit(solution)/shard_map/attend/pallas_call | solution.py:465
  39.5 2.4 %collective-permute-start.12 = (bf16[32,1280]{1,0:T(8,128)(2,1)S(1)}, bf16[32,1280]{1,0:T(8,128)(2,1)S(1)}, u32[]{:S(2)}, u32[]{:S(2)}) collective-permute-start(bf16[32,1280]{1,0:T(8,128)(2,1)S(1)} %get-tuple-element.60), channel_id=1, source_target_pairs={{0,3},{1,2},{2,1},{3,0},{4,7},{5,6},{6,5},{7,4},{8,11},{9,10},{10,... | collective-permute-start | bytes 245768 | tf_op jit(solution)/shard_map/ppermute | solution.py:408
  41.9 0.8 %collective-permute-start.13 = (bf16[32,1280]{1,0:T(8,128)(2,1)S(1)}, bf16[32,1280]{1,0:T(8,128)(2,1)S(1)}, u32[]{:S(2)}, u32[]{:S(2)}) collective-permute-start(bf16[32,1280]{1,0:T(8,128)(2,1)S(1)} %get-tuple-element.61), channel_id=1, source_target_pairs={{0,2},{1,3},{2,0},{3,1},{4,6},{5,7},{6,4},{7,5},{8,10},{9,11},{10,... | collective-permute-start | bytes 245768 | tf_op jit(solution)/shard_map/ppermute | solution.py:408
  42.7 1.0 %collective-permute-start.14 = (bf16[32,1280]{1,0:T(8,128)(2,1)S(1)}, bf16[32,1280]{1,0:T(8,128)(2,1)S(1)}, u32[]{:S(2)}, u32[]{:S(2)}) collective-permute-start(bf16[32,1280]{1,0:T(8,128)(2,1)S(1)} %get-tuple-element.62), channel_id=1, source_target_pairs={{0,1},{1,0},{2,3},{3,2},{4,5},{5,4},{6,7},{7,6},{8,9},{9,8},{10,11... | collective-permute-start | bytes 245768 | tf_op jit(solution)/shard_map/ppermute | solution.py:408
  43.7 2.0 %collective-permute-done.12.refs_1_ = bf16[32,1280]{1,0:T(8,128)(2,1)S(1)} collective-permute-done((bf16[32,1280]{1,0:T(8,128)(2,1)S(1)}, bf16[32,1280]{1,0:T(8,128)(2,1)S(1)}, u32[]{:S(2)}, u32[]{:S(2)}) %collective-permute-start.12) | collective-permute-done | bytes 81952 | tf_op jit(solution)/shard_map/ppermute | solution.py:408
  45.7 3.0 %collective-permute-done.13.refs_2_ = bf16[32,1280]{1,0:T(8,128)(2,1)S(1)} collective-permute-done((bf16[32,1280]{1,0:T(8,128)(2,1)S(1)}, bf16[32,1280]{1,0:T(8,128)(2,1)S(1)}, u32[]{:S(2)}, u32[]{:S(2)}) %collective-permute-start.13) | collective-permute-done | bytes 81952 | tf_op jit(solution)/shard_map/ppermute | solution.py:408
  48.7 0.0 collective-permute-done.14.refs_3_
  48.7 0.8 %place.1 = bf16[32,5120]{1,0:T(8,128)(2,1)} custom-call(bf16[32,1280]{1,0:T(8,128)(2,1)S(1)} %get-tuple-element.59.refs_0_, bf16[32,1280]{1,0:T(8,128)(2,1)S(1)} %collective-permute-done.12.refs_1_, bf16[32,1280]{1,0:T(8,128)(2,1)S(1)} %collective-permute-done.13.refs_2_, bf16[32,1280]{1,0:T(8,128)(2,1)S(1)} %collective-permute-done.14.refs_3_), custom_call_target="tpu_custom_call" | custom-call | tf_op jit(solution)/shard_map/place/pallas_call | solution.py:480
  (1 shorter events, 0.0 us)
Async XLA Ops:
  3.2 10.2 %collective-permute-start = (bf16[32,2560]{1,0:T(8,128)(2,1)}, bf16[32,2560]{1,0:T(8,128)(2,1)S(1)}, u32[]{:S(2)}, u32[]{:S(2)}) collective-permute-start(bf16[32,2560]{1,0:T(8,128)(2,1)} %get-tuple-element.35), channel_id=1, source_target_pairs={{0,3},{1,2},{2,1},{3,0},{4,7},{5,6},{6,5},{7,4},{8,11},{9,10},{10,... | collective-permute-start | bytes 491528 | tf_op jit(solution)/shard_map/ppermute | solution.py:408
  6.1 8.8 %collective-permute-start.1 = (bf16[32,2560]{1,0:T(8,128)(2,1)}, bf16[32,2560]{1,0:T(8,128)(2,1)S(1)}, u32[]{:S(2)}, u32[]{:S(2)}) collective-permute-start(bf16[32,2560]{1,0:T(8,128)(2,1)} %get-tuple-element.36), channel_id=1, source_target_pairs={{0,2},{1,3},{2,0},{3,1},{4,6},{5,7},{6,4},{7,5},{8,10},{9,11},{10,... | collective-permute-start | bytes 491528 | tf_op jit(solution)/shard_map/ppermute | solution.py:408
  6.9 9.4 %collective-permute-start.2 = (bf16[32,2560]{1,0:T(8,128)(2,1)}, bf16[32,2560]{1,0:T(8,128)(2,1)S(1)}, u32[]{:S(2)}, u32[]{:S(2)}) collective-permute-start(bf16[32,2560]{1,0:T(8,128)(2,1)} %get-tuple-element.37), channel_id=1, source_target_pairs={{0,1},{1,0},{2,3},{3,2},{4,5},{5,4},{6,7},{7,6},{8,9},{9,8},{10,11... | collective-permute-start | bytes 491528 | tf_op jit(solution)/shard_map/ppermute | solution.py:408
  7.4 9.8 %collective-permute-start.3 = (bf16[16,5120]{1,0:T(8,128)(2,1)}, bf16[16,5120]{1,0:T(8,128)(2,1)S(1)}, u32[]{:S(2)}, u32[]{:S(2)}) collective-permute-start(bf16[16,5120]{1,0:T(8,128)(2,1)} %get-tuple-element.38), channel_id=1, source_target_pairs={{16,0},{17,1},{18,2},{19,3},{20,4},{21,5},{22,6},{23,7},{24,8},{25... | collective-permute-start | bytes 491528 | tf_op jit(solution)/shard_map/ppermute | solution.py:404
  8.6 9.7 %collective-permute-start.4 = (bf16[16,5120]{1,0:T(8,128)(2,1)}, bf16[16,5120]{1,0:T(8,128)(2,1)S(1)}, u32[]{:S(2)}, u32[]{:S(2)}) collective-permute-start(bf16[16,5120]{1,0:T(8,128)(2,1)} %get-tuple-element.38), channel_id=1, source_target_pairs={{1,0},{0,1},{3,2},{2,3},{5,4},{4,5},{7,6},{6,7},{9,8},{8,9},{11,10... | collective-permute-start | bytes 491528 | tf_op jit(solution)/shard_map/ppermute | solution.py:404
  16.2 0.9 %copy-start.1 = (bf16[32,2560]{1,0:T(8,128)(2,1)S(1)}, bf16[32,2560]{1,0:T(8,128)(2,1)}, u32[]{:S(2)}) copy-start(bf16[32,2560]{1,0:T(8,128)(2,1)} %get-tuple-element.34.refs_0_) | copy-start | bytes 491524
  17.1 3.3 %copy-start = (bf16[4,32,1280]{2,1,0:T(8,128)(2,1)S(1)}, bf16[4,32,1280]{2,1,0:T(8,128)(2,1)}, u32[]{:S(2)}) copy-start(bf16[4,32,1280]{2,1,0:T(8,128)(2,1)} %get-tuple-element.44.q_ref) | copy-start | bytes 983044
  18.3 2.1 %collective-permute-start.6 = (bf16[128,2560]{1,0:T(8,128)(2,1)S(1)}, bf16[128,2560]{1,0:T(8,128)(2,1)S(1)}, u32[]{:S(2)}, u32[]{:S(2)}) collective-permute-start(bf16[128,2560]{1,0:T(8,128)(2,1)S(1)} %assemble.1.own_ref), channel_id=1, source_target_pairs={{4,0},{5,1},{6,2},{7,3},{0,4},{1,5},{2,6},{3,7},{12,8},{13,9},{14,... | collective-permute-start | bytes 1966088 | tf_op jit(solution)/shard_map/ppermute | solution.py:404
  18.3 11.0 %collective-permute-start.5 = (bf16[128,2560]{1,0:T(8,128)(2,1)S(1)}, bf16[128,2560]{1,0:T(8,128)(2,1)S(1)}, u32[]{:S(2)}, u32[]{:S(2)}) collective-permute-start(bf16[128,2560]{1,0:T(8,128)(2,1)S(1)} %assemble.1.own_ref), channel_id=1, source_target_pairs={{1,0},{0,1},{3,2},{2,3},{8,4},{9,5},{10,6},{11,7},{4,8},{5,9},{6,1... | collective-permute-start | bytes 1966088 | tf_op jit(solution)/shard_map/ppermute | solution.py:404
  20.4 8.8 %collective-permute-start.7 = (bf16[64,1280]{1,0:T(8,128)(2,1)S(1)}, bf16[64,1280]{1,0:T(8,128)(2,1)S(1)}, u32[]{:S(2)}, u32[]{:S(2)}) collective-permute-start(bf16[64,1280]{1,0:T(8,128)(2,1)S(1)} %get-tuple-element.46), channel_id=1, source_target_pairs={{0,3},{1,2},{2,1},{3,0},{4,7},{5,6},{6,5},{7,4},{8,11},{9,10},{10,... | collective-permute-start | bytes 491528 | tf_op jit(solution)/shard_map/ppermute | solution.py:408
  23.3 1.3 %copy-start.2 = (s32[64]{0:T(128)S(1)}, s32[64]{0:T(128)}, u32[]{:S(2)}) copy-start(s32[64]{0:T(128)} %param.16) | copy-start | bytes 772
  23.3 8.6 %collective-permute-start.8 = (bf16[64,1280]{1,0:T(8,128)(2,1)S(1)}, bf16[64,1280]{1,0:T(8,128)(2,1)S(1)}, u32[]{:S(2)}, u32[]{:S(2)}) collective-permute-start(bf16[64,1280]{1,0:T(8,128)(2,1)S(1)} %get-tuple-element.47), channel_id=1, source_target_pairs={{0,2},{1,3},{2,0},{3,1},{4,6},{5,7},{6,4},{7,5},{8,10},{9,11},{10,... | collective-permute-start | bytes 491528 | tf_op jit(solution)/shard_map/ppermute | solution.py:408
  24.1 9.2 %collective-permute-start.9 = (bf16[64,1280]{1,0:T(8,128)(2,1)S(1)}, bf16[64,1280]{1,0:T(8,128)(2,1)S(1)}, u32[]{:S(2)}, u32[]{:S(2)}) collective-permute-start(bf16[64,1280]{1,0:T(8,128)(2,1)S(1)} %get-tuple-element.48), channel_id=1, source_target_pairs={{0,1},{1,0},{2,3},{3,2},{4,5},{5,4},{6,7},{7,6},{8,9},{9,8},{10,11... | collective-permute-start | bytes 491528 | tf_op jit(solution)/shard_map/ppermute | solution.py:408
  25.0 11.8 %collective-permute-start.10 = (bf16[64,2560]{1,0:T(8,128)(2,1)S(1)}, bf16[64,2560]{1,0:T(8,128)(2,1)S(1)}, u32[]{:S(2)}, u32[]{:S(2)}) collective-permute-start(bf16[64,2560]{1,0:T(8,128)(2,1)S(1)} %pool.1), channel_id=1, source_target_pairs={{4,0},{5,1},{6,2},{7,3},{12,4},{13,5},{14,6},{15,7},{0,8},{1,9},{2... | collective-permute-start | bytes 983048 | tf_op jit(solution)/shard_map/ppermute | solution.py:404
  33.3 2.9 %copy-start.3 = (s32[1,64]{1,0:T(1,128)S(1)}, s32[1,64]{1,0:T(1,128)}, u32[]{:S(2)}) copy-start(s32[1,64]{1,0:T(1,128)} %keep_ref.1) | copy-start | bytes 772
  33.3 2.9 %copy-start.4 = (s32[1,64]{1,0:T(1,128)S(1)}, s32[1,64]{1,0:T(1,128)}, u32[]{:S(2)}) copy-start(s32[1,64]{1,0:T(1,128)} %level_ref.1) | copy-start | bytes 772
  33.6 3.8 %collective-permute-start.11 = (bf16[64,2560]{1,0:T(8,128)(2,1)S(1)}, bf16[64,2560]{1,0:T(8,128)(2,1)S(1)}, u32[]{:S(2)}, u32[]{:S(2)}) collective-permute-start(bf16[64,2560]{1,0:T(8,128)(2,1)S(1)} %pool_cross.1), channel_id=1, source_target_pairs={{4,0},{5,1},{6,2},{7,3},{0,4},{1,5},{2,6},{3,7},{12,8},{13,9},{14,... | collective-permute-start | bytes 983048 | tf_op jit(solution)/shard_map/ppermute | solution.py:404
  39.5 6.2 %collective-permute-start.12 = (bf16[32,1280]{1,0:T(8,128)(2,1)S(1)}, bf16[32,1280]{1,0:T(8,128)(2,1)S(1)}, u32[]{:S(2)}, u32[]{:S(2)}) collective-permute-start(bf16[32,1280]{1,0:T(8,128)(2,1)S(1)} %get-tuple-element.60), channel_id=1, source_target_pairs={{0,3},{1,2},{2,1},{3,0},{4,7},{5,6},{6,5},{7,4},{8,11},{9,10},{10,... | collective-permute-start | bytes 245768 | tf_op jit(solution)/shard_map/ppermute | solution.py:408
  41.9 6.8 %collective-permute-start.13 = (bf16[32,1280]{1,0:T(8,128)(2,1)S(1)}, bf16[32,1280]{1,0:T(8,128)(2,1)S(1)}, u32[]{:S(2)}, u32[]{:S(2)}) collective-permute-start(bf16[32,1280]{1,0:T(8,128)(2,1)S(1)} %get-tuple-element.61), channel_id=1, source_target_pairs={{0,2},{1,3},{2,0},{3,1},{4,6},{5,7},{6,4},{7,5},{8,10},{9,11},{10,... | collective-permute-start | bytes 245768 | tf_op jit(solution)/shard_map/ppermute | solution.py:408
  42.7 6.0 %collective-permute-start.14 = (bf16[32,1280]{1,0:T(8,128)(2,1)S(1)}, bf16[32,1280]{1,0:T(8,128)(2,1)S(1)}, u32[]{:S(2)}, u32[]{:S(2)}) collective-permute-start(bf16[32,1280]{1,0:T(8,128)(2,1)S(1)} %get-tuple-element.62), channel_id=1, source_target_pairs={{0,1},{1,0},{2,3},{3,2},{4,5},{5,4},{6,7},{7,6},{8,9},{9,8},{10,11... | collective-permute-start | bytes 245768 | tf_op jit(solution)/shard_map/ppermute | solution.py:408
